TPU v7x, 32 devices: a whole 2x2x4 slice. The times are simulated.
32 devices in a mesh: groups: 2 (over y), expert: 8 (over z, x), dp: 2 (over core).
Axes of the slice: x: 2, y: 2, z: 4, core: 2. Of those that a mesh axis runs over, the one named last changes fastest.
Arguments:
- grad_out: bfloat16 [4096, 2048], P(('groups', 'expert', 'dp')), parts along dimension 0, may hold values from -3 to 3
- pre_act: bfloat16 [4096, 2, 2, 512], P(('groups', 'expert', 'dp')), parts along dimension 0, may hold values from -6 to 6
- routes: int32 [4096, 2], P(('groups', 'expert', 'dp')), parts along dimension 0, may hold values from 0 to 7, all different within a row; in each aligned block of 128 rows (0 to 127, 128 to 255, ...) at most 128 rows name the same one
- gate_prob: float32 [4096, 2], P(('groups', 'expert', 'dp')), parts along dimension 0, may hold values from 0.1 to 1
- down_weight: bfloat16 [8, 512, 2048], P('expert', 'dp'), may hold values from -0.25 to 0.25
Outputs:
- d_pre: bfloat16 [4096, 2, 2, 512], P(('groups', 'expert', 'dp')), parts along dimension 0
- grad_down: bfloat16 [16, 512, 2048], P(('groups', 'expert'), 'dp'), parts along dimension 0
There are 2 independent parts, one for each index of `groups`. A program takes and returns all parts, laid end to end along the dimension named above; an argument that names none is the same for every part. Nothing has to cross between parts.
Inputs may be any that keep to these rules, and one draw needn't show every extreme that they name: Each token names 2 different experts. Within the 128 tokens of one device, each expert is named by at most 128 routes, a bound that some block reaches.
All inputs are finite; a program needn't handle non-finite values.
Results may differ from a plain program's by a relative error of at most 0.0065.
Values may be sent and summed in bfloat16 or wider, within the bound.
A program may use at most 64 MiB of HBM per device.

v0:
```python
import jax
import jax.numpy as jnp
from jax import lax
from jax.sharding import PartitionSpec as P


def gate_hidden(gate_pre, up_pre):
    sigmoid_gate = jax.nn.sigmoid(gate_pre)
    return (gate_pre * sigmoid_gate * up_pre).astype(jnp.bfloat16)


def activation_grads(hidden_grad, gate_pre, up_pre):
    sigmoid_gate = jax.nn.sigmoid(gate_pre)
    upstream = hidden_grad.astype(jnp.float32)
    gate_part = upstream * up_pre * sigmoid_gate * (1.0 + gate_pre * (1.0 - sigmoid_gate))
    up_part = upstream * (gate_pre * sigmoid_gate)
    return jnp.concatenate([gate_part, up_part], axis=-1).astype(jnp.bfloat16)


def pack_rows(row_values, slot_index, peer_count, capacity):
    row_width = row_values.shape[1]
    buffer = (
        jnp.zeros((peer_count * capacity, row_width), row_values.dtype)
        .at[slot_index]
        .set(row_values)
    )
    return buffer.reshape(peer_count, capacity, row_width)


def expert_work(scaled_rows, hidden_rows, full_weight):
    dims_back = (((1,), (1,)), ((), ()))
    dims_outer = (((0,), (0,)), ((), ()))
    hidden_grad = lax.dot_general(
        scaled_rows, full_weight, dims_back, preferred_element_type=jnp.float32
    ).astype(jnp.bfloat16)
    partial_value = lax.dot_general(
        hidden_rows, scaled_rows, dims_outer, preferred_element_type=jnp.float32
    )
    return (hidden_grad, partial_value)


def balanced_work(got_scaled, got_hidden, full_weight):
    peer_count = got_scaled.shape[0]
    capacity = got_scaled.shape[1]
    slots_all = peer_count * capacity
    scaled_rows = got_scaled.reshape(slots_all, got_scaled.shape[2])
    hidden_rows = got_hidden.reshape(slots_all, got_hidden.shape[2])
    hidden_grad, partial_value = expert_work(scaled_rows, hidden_rows, full_weight)
    return (hidden_grad.reshape(peer_count, capacity, hidden_grad.shape[1]), partial_value)


def shards(grad_out, pre_act, routes, gate_prob, down_weight):
    peer_count = lax.axis_size("expert")
    token_rows = routes.shape[0]
    route_width = routes.shape[1]
    route_count = token_rows * route_width
    capacity = 4 * route_count // peer_count
    feature_count = grad_out.shape[1]
    hidden_count = pre_act.shape[3]
    scaled = (
        (gate_prob[:, :, None] * grad_out[:, None, :].astype(jnp.float32))
        .astype(jnp.bfloat16)
        .reshape(route_count, feature_count)
    )
    pre_rows = pre_act.reshape(route_count, 2 * hidden_count)
    expert_ids = routes.reshape(route_count)
    one_hot = (expert_ids[:, None] == jnp.arange(peer_count, dtype=jnp.int32)[None, :]).astype(
        jnp.int32
    )
    slot_rank = jnp.sum(jnp.cumsum(one_hot, axis=0) * one_hot, axis=1) - 1
    sent_counts = jnp.sum(one_hot, axis=0).reshape(peer_count, 1)
    slot_index = expert_ids * capacity + slot_rank
    full_weight = lax.all_gather(down_weight[0], "dp", axis=0, tiled=True)
    got_scaled, got_pre, arrived = (
        lax.all_to_all(
            pack_rows(scaled, slot_index, peer_count, capacity),
            "expert",
            split_axis=0,
            concat_axis=0,
            tiled=True,
        ),
        lax.all_to_all(
            pack_rows(pre_rows, slot_index, peer_count, capacity),
            "expert",
            split_axis=0,
            concat_axis=0,
            tiled=True,
        ),
        lax.all_to_all(sent_counts, "expert", split_axis=0, concat_axis=0, tiled=True),
    )
    pre_float = got_pre.astype(jnp.float32)
    gate_pre = pre_float[:, :, :hidden_count]
    up_pre = pre_float[:, :, hidden_count:]
    got_hidden = gate_hidden(gate_pre, up_pre)
    hidden_grad, partial_value = balanced_work(got_scaled, got_hidden, full_weight)
    slot_grads = activation_grads(hidden_grad, gate_pre, up_pre)
    returned = lax.all_to_all(slot_grads, "expert", split_axis=0, concat_axis=0, tiled=True)
    d_pre = returned.reshape(peer_count * capacity, 2 * hidden_count)[slot_index]
    summed = lax.psum_scatter(
        partial_value.astype(jnp.bfloat16), "dp", scatter_dimension=0, tiled=True
    )
    return (d_pre.reshape(token_rows, route_width, 2, hidden_count), summed[None])


def solution(mesh):
    placed = (
        P(("groups", "expert", "dp"), None),
        P(("groups", "expert", "dp"), None, None, None),
        P(("groups", "expert", "dp"), None),
        P(("groups", "expert", "dp"), None),
        P("expert", "dp", None),
    )
    return jax.shard_map(
        shards,
        mesh=mesh,
        in_specs=placed,
        out_specs=(
            P(("groups", "expert", "dp"), None, None, None),
            P(("groups", "expert"), "dp", None),
        ),
        check_vma=False,
    )
```

profile of v0, /device:TPU:0, one launch (start us, length us, event | category | flops | bytes accessed | tf_op | source)
XLA Modules:
  0.0 244.1 jit_solution(14576698673156907168)
XLA Ops:
  7.2 0.8 copy.11
  8.0 0.1 eq.29
  8.1 0.1 eq.25
  8.2 0.7 broadcast_multiply_fusion
  8.9 0.6 reduce-window.6
  9.5 0.2 slice_reduce_fusion
  9.7 0.1 fusion.16
  9.8 0.1 copy.10
  10.0 0.1 mul.61
  10.1 1.1 copy.16
  11.2 3.2 %scatter_custom_fusion.1 = bf16[1024,1024]{1,0:T(8,128)(2,1)} fusion(s32[256]{0:T(256)S(1)} %bitcast.33, bf16[256,1024]{1,0:T(8,128)(2,1)S(1)} %bitcast.32, bf16[]{:T(256)} %constant.6.clone.1), kind=kCustom, calls=%fused_computation.20 | custom fusion | bytes 2097154 | tf_op jit(solution)/shard_map/scatter | solution.py:25
  14.5 7.4 %all-to-all-start.1 = ((bf16[8,128,1024]{2,1,0:T(8,128)(2,1)}), bf16[8,128,1024]{2,1,0:T(8,128)(2,1)S(1)}, u32[]{:S(2)}, u32[]{:S(2)}) async-start(bf16[8,128,1024]{2,1,0:T(8,128)(2,1)} %bitcast.29), calls=%async_computation.1 | async-start | bytes 4194304 | tf_op jit(solution)/shard_map/all_to_all | solution.py:82
  21.9 2.4 mul.65
  24.3 3.7 %mul.66 = f32[256,2048]{1,0:T(8,128)} reshape(f32[128,2,2048]{2,1,0:T(2,128)} %mul.65) | data formatting | bytes 4194304 | tf_op jit(solution)/shard_map/mul | solution.py:61
  27.9 0.1 copy.13
  28.1 0.1 mul.63
  28.2 5.9 %scatter_custom_fusion = bf16[1024,2048]{1,0:T(8,128)(2,1)} fusion(s32[256]{0:T(256)S(1)} %bitcast.34, bf16[]{:T(256)} %constant.6.clone.1, f32[256,2048]{1,0:T(8,128)} %mul.66, f32[256]{0:T(256)S(1)} %mul.63), kind=kCustom, calls=%fused_computation.17 | custom fusion | flops 1048576 | bytes 6292482 | tf_op jit(solution)/shard_map/scatter | solution.py:25
  34.1 36.0 %all-to-all-done.1 = bf16[8,128,1024]{2,1,0:T(8,128)(2,1)S(1)} async-done(((bf16[8,128,1024]{2,1,0:T(8,128)(2,1)}), bf16[8,128,1024]{2,1,0:T(8,128)(2,1)S(1)}, u32[]{:S(2)}, u32[]{:S(2)}) %all-to-all-start.1) | async-done | bytes 2097184 | tf_op jit(solution)/shard_map/all_to_all | solution.py:82
  70.1 4.5 %all-to-all-start = ((bf16[8,128,2048]{2,1,0:T(8,128)(2,1)}), bf16[8,128,2048]{2,1,0:T(8,128)(2,1)}, u32[]{:S(2)}, u32[]{:S(2)}) async-start(bf16[8,128,2048]{2,1,0:T(8,128)(2,1)} %bitcast.28), calls=%async_computation | async-start | bytes 8388608 | tf_op jit(solution)/shard_map/all_to_all | solution.py:75
  74.7 0.0 all-gather.3.cloned.1.call-start
  74.7 0.7 all-gather.3.cloned.1.call-update
  75.4 0.2 reduce-scatter.2.cloned.1.call-start
  75.6 2.4 %convert_element_type.38 = f32[8,128,1024]{2,1,0:T(8,128)} convert(bf16[8,128,1024]{2,1,0:T(8,128)(2,1)S(1)} %all-to-all-done.1) | non-fusion elementwise | flops 1048576 | bytes 6291456 | tf_op jit(solution)/shard_map/convert_element_type | solution.py:91
  78.1 89.2 %all-to-all-done = bf16[8,128,2048]{2,1,0:T(8,128)(2,1)} async-done(((bf16[8,128,2048]{2,1,0:T(8,128)(2,1)}), bf16[8,128,2048]{2,1,0:T(8,128)(2,1)}, u32[]{:S(2)}, u32[]{:S(2)}) %all-to-all-start) | async-done | bytes 4194336 | tf_op jit(solution)/shard_map/all_to_all | solution.py:75
  167.2 7.3 %bitcast_convert_fusion = bf16[512,2048]{1,0:T(8,128)(2,1)} fusion(bf16[8,128,2048]{2,1,0:T(8,128)(2,1)} %all-to-all-done, f32[8,128,1024]{2,1,0:T(8,128)} %convert_element_type.38), kind=kOutput, calls=%fused_computation.3 | convolution fusion | flops 2151677952 | bytes 10485760 | tf_op jit(solution)/shard_map/dot_general | solution.py:36
  174.6 5.4 %fusion.9 = bf16[1024,512]{1,0:T(8,128)(2,1)S(1)} fusion(bf16[1024,2048]{1,0:T(8,128)(2,1)} %bitcast.5, bf16[1,512,2048]{2,1,0:T(8,128)(2,1)} %all-gather.3.cloned.1.call-done), kind=kOutput, calls=%fused_computation.19 | convolution fusion | flops 2148007936 | bytes 7340032 | tf_op jit(solution)/shard_map/dot_general | solution.py:33
  180.0 1.3 fusion.2
  181.3 1.6 pad_maximum_fusion
  182.9 3.6 %all-to-all-start.2 = ((bf16[8,128,1024]{2,1,0:T(8,128)(2,1)}), bf16[8,128,1024]{2,1,0:T(8,128)(2,1)S(1)}, u32[]{:S(2)}, u32[]{:S(2)}) async-start(bf16[8,128,1024]{2,1,0:T(8,128)(2,1)} %pad_maximum_fusion), calls=%async_computation.2 | async-start | bytes 4194304 | tf_op jit(solution)/shard_map/all_to_all | solution.py:97
  186.5 48.4 %all-to-all-done.2 = bf16[8,128,1024]{2,1,0:T(8,128)(2,1)S(1)} async-done(((bf16[8,128,1024]{2,1,0:T(8,128)(2,1)}), bf16[8,128,1024]{2,1,0:T(8,128)(2,1)S(1)}, u32[]{:S(2)}, u32[]{:S(2)}) %all-to-all-start.2) | async-done | bytes 2097184 | tf_op jit(solution)/shard_map/all_to_all | solution.py:97
  234.9 1.2 gather_fusion
  236.1 1.2 reshape.90
  (15 shorter events, 0.1 us)
Async XLA Ops:
  14.5 7.4 %copy-start.1 = (bf16[128,2048]{1,0:T(8,128)(2,1)S(1)}, bf16[128,2048]{1,0:T(8,128)(2,1)}, u32[]{:S(2)}) copy-start(bf16[128,2048]{1,0:T(8,128)(2,1)} %param.5) | copy-start | bytes 1572868
  14.5 55.6 %all-to-all-start.1 = ((bf16[8,128,1024]{2,1,0:T(8,128)(2,1)}), bf16[8,128,1024]{2,1,0:T(8,128)(2,1)S(1)}, u32[]{:S(2)}, u32[]{:S(2)}) async-start(bf16[8,128,1024]{2,1,0:T(8,128)(2,1)} %bitcast.29), calls=%async_computation.1 | async-start | bytes 4194304 | tf_op jit(solution)/shard_map/all_to_all | solution.py:82
  24.3 3.7 %copy-start.2 = (f32[128,2]{0,1:T(2,128)S(1)}, f32[128,2]{0,1:T(2,128)}, u32[]{:S(2)}) copy-start(f32[128,2]{0,1:T(2,128)} %param.8) | copy-start | bytes 3076
  70.1 97.1 %all-to-all-start = ((bf16[8,128,2048]{2,1,0:T(8,128)(2,1)}), bf16[8,128,2048]{2,1,0:T(8,128)(2,1)}, u32[]{:S(2)}, u32[]{:S(2)}) async-start(bf16[8,128,2048]{2,1,0:T(8,128)(2,1)} %bitcast.28), calls=%async_computation | async-start | bytes 8388608 | tf_op jit(solution)/shard_map/all_to_all | solution.py:75
  74.7 99.9 %all-gather.3.cloned.1.call-start = ((), (), s32[]{:S(2)}) async-start(), calls=%async_computation.5 | async-start | bytes 3145728 | tf_op jit(solution)/shard_map/all_gather | solution.py:73
  75.4 161.8 %reduce-scatter.2.cloned.1.call-start = ((), (), s32[]{:S(2)}) async-start(), calls=%async_computation.4 | async-start | bytes 3145728 | tf_op jit(solution)/shard_map/reduce_scatter | solution.py:99
  174.6 5.4 %copy-start = (f32[8,128,1024]{2,1,0:T(8,128)S(1)}, f32[8,128,1024]{2,1,0:T(8,128)}, u32[]{:S(2)}) copy-start(f32[8,128,1024]{2,1,0:T(8,128)} %convert_element_type.38) | copy-start | bytes 12582916
  182.9 52.0 %all-to-all-start.2 = ((bf16[8,128,1024]{2,1,0:T(8,128)(2,1)}), bf16[8,128,1024]{2,1,0:T(8,128)(2,1)S(1)}, u32[]{:S(2)}, u32[]{:S(2)}) async-start(bf16[8,128,1024]{2,1,0:T(8,128)(2,1)} %pad_maximum_fusion), calls=%async_computation.2 | async-start | bytes 4194304 | tf_op jit(solution)/shard_map/all_to_all | solution.py:97
Sparse Core Ops, SparseCore 0:
  77.0 11.9 all-gather.2
  174.7 8.6 reduce-scatter.1
where the time goes:
time: 245 us; the launch traced here: 244 us
  waiting for transfers between devices  174 us (71%)
  starting transfers between devices  15.8 us (6%)
  local copies, waits for them, and re-layouts  14.6 us (6%)
  between operations  14.1 us (6%)
  matrix products  12.7 us (5%)
  other arithmetic  12.6 us (5%)
    all_to_all x1, waiting for transfers between devices, shards(): lax.all_to_all(pack_rows(scaled, slot_index, peer_count, capacity), 'expe...  89.2 us
    all_to_all x1, waiting for transfers between devices, shards(): lax.all_to_all(slot_grads, 'expert', split_axis=0, concat_axis=0, tiled=T...  48.4 us
    all_to_all x1, waiting for transfers between devices, shards(): lax.all_to_all(pack_rows(pre_rows, slot_index, peer_count, capacity), 'ex...  36 us
    all_to_all x1, starting transfers between devices, shards(): lax.all_to_all(pack_rows(pre_rows, slot_index, peer_count, capacity), 'ex...  7.38 us
    dot_general x1, matrix products, expert_work(): lax.dot_general(hidden_rows, scaled_rows, dims_outer, preferred_element_t...  7.32 us
    mul x3, local copies, waits for them, and re-layouts, shards(): gate_prob[:, :, None] * grad_out[:, None, :].astype(jnp.float32)  6.21 us
    scatter x1, other arithmetic, pack_rows(): buffer = jnp.zeros((peer_count * capacity, row_width), row_values.dtype)....  5.91 us
    dot_general x1, matrix products, expert_work(): lax.dot_general(scaled_rows, full_weight, dims_back, preferred_element_ty...  5.36 us
  transfers between devices with their start and end apart: 5, of which 3 were waited for; matrix products, arithmetic and copies ran while one was open for 13% of the time, Pallas kernels for 0%

commit v1 on v0

--- a/solution.py
+++ b/solution.py
@@ -49,7 +49,7 @@
     return (hidden_grad.reshape(peer_count, capacity, hidden_grad.shape[1]), partial_value)
 
 
-def shards(grad_out, pre_act, routes, gate_prob, down_weight):
+def packed_shards(grad_out, pre_act, routes, gate_prob, down_weight):
     peer_count = lax.axis_size("expert")
     token_rows = routes.shape[0]
     route_width = routes.shape[1]
@@ -102,6 +102,53 @@
     return (d_pre.reshape(token_rows, route_width, 2, hidden_count), summed[None])
 
 
+def dense_shards(grad_out, pre_act, routes, gate_prob, down_weight):
+    peer_count = lax.axis_size("expert")
+    me = lax.axis_index("expert")
+    token_rows, feature_count = grad_out.shape
+    hidden_count = pre_act.shape[3]
+    pre_float = pre_act.astype(jnp.float32)
+    gate_pre, up_pre = pre_float[:, :, 0, :], pre_float[:, :, 1, :]
+    hidden = gate_hidden(gate_pre, up_pre).reshape(token_rows, 2 * hidden_count)
+    all_routes = lax.all_gather(routes, "expert", axis=0, tiled=True)
+    all_prob = lax.all_gather(gate_prob, "expert", axis=0, tiled=True)
+    all_grad = lax.all_gather(grad_out, "expert", axis=0, tiled=True)
+    all_hidden = lax.all_gather(hidden, "expert", axis=0, tiled=True)
+    full_weight = lax.all_gather(down_weight[0], "dp", axis=0, tiled=True)
+    mine = all_routes == me
+    factor = jnp.sum(jnp.where(mine, all_prob, 0.0), axis=1, keepdims=True)
+    scaled_rows = (factor * all_grad.astype(jnp.float32)).astype(jnp.bfloat16)
+    hidden_rows = jnp.where(
+        mine[:, :1],
+        all_hidden[:, :hidden_count],
+        jnp.where(mine[:, 1:], all_hidden[:, hidden_count:], jnp.zeros((), jnp.bfloat16)),
+    )
+    hidden_grad, partial_value = expert_work(scaled_rows, hidden_rows, full_weight)
+    returned = lax.all_to_all(
+        hidden_grad.reshape(peer_count, token_rows, hidden_count),
+        "expert",
+        split_axis=0,
+        concat_axis=0,
+        tiled=True,
+    )
+    summed = lax.psum_scatter(
+        partial_value.astype(jnp.bfloat16), "dp", scatter_dimension=0, tiled=True
+    )
+    picked = jnp.zeros((token_rows, 2, hidden_count), jnp.bfloat16)
+    for expert in range(peer_count):
+        picked = jnp.where(
+            (routes == expert)[:, :, None], returned[expert][:, None, :], picked
+        )
+    d_pre = activation_grads(picked, gate_pre, up_pre)
+    return (d_pre.reshape(token_rows, 2, 2, hidden_count), summed[None])
+
+
+def shards(grad_out, pre_act, routes, gate_prob, down_weight):
+    capacity = 4 * routes.shape[0] * routes.shape[1] // lax.axis_size("expert")
+    plan = dense_shards if capacity >= routes.shape[0] else packed_shards
+    return plan(grad_out, pre_act, routes, gate_prob, down_weight)
+
+
 def solution(mesh):
     placed = (
         P(("groups", "expert", "dp"), None),

time: 245 us -> 197 us (0.80)
  waiting for transfers between devices: 174 us -> 120 us
  blocking collectives: 0 us -> 38.6 us
  other arithmetic: 12.6 us -> 1.46 us
  local copies, waits for them, and re-layouts: 14.6 us -> 3.72 us
  starting transfers between devices: 15.8 us -> 5.92 us
    all_to_all x3 -> x1, waiting for transfers between devices: 174 us -> 26.1 us  [dense_shards(): lax.all_to_all(hidden_grad.reshape(peer_count, token_rows, hidden_count),...]
    all_gather x1 -> x3, waiting for transfers between devices: 0.02 us -> 92.2 us  [the longest x1 73.8 us: dense_shards(): all_grad = lax.all_gather(grad_out, 'expert', axis=0, tiled=True)]
    all_gather x0 -> x2, blocking collectives: none -> 38.6 us  [the longest x1 22.2 us: dense_shards(): all_prob = lax.all_gather(gate_prob, 'expert', axis=0, tiled=True)]
    all_to_all x3 -> x1, starting transfers between devices: 15.6 us -> 5.77 us  [dense_shards(): lax.all_to_all(hidden_grad.reshape(peer_count, token_rows, hidden_count),...]
    mul x5 -> x0, local copies, waits for them, and re-layouts: 6.47 us -> none  [the longest x3 6.21 us: shards(): gate_prob[:, :, None] * grad_out[:, None, :].astype(jnp.float32)]
    scatter x1 -> x0, other arithmetic: 5.91 us -> none  [pack_rows(): buffer = jnp.zeros((peer_count * capacity, row_width), row_values.dtype)....]
    scatter x1 -> x0, local copies, waits for them, and re-layouts: 3.24 us -> none  [pack_rows(): buffer = jnp.zeros((peer_count * capacity, row_width), row_values.dtype)....]
  transfers between devices with their start and end apart: 5 -> 5, of which waited for: 3 -> 4; matrix products, arithmetic and copies ran while one was open for 13% -> 8% of each run, Pallas kernels for 0% -> 0%
where the time goes in v1:
time: 197 us; the launch traced here: 196 us
  waiting for transfers between devices  120 us (61%)
  blocking collectives  38.6 us (20%)
  between operations  13.9 us (7%)
  matrix products  12.9 us (7%)
  starting transfers between devices  5.92 us (3%)
  local copies, waits for them, and re-layouts  3.72 us (2%)
    all_gather x1, waiting for transfers between devices, dense_shards(): all_grad = lax.all_gather(grad_out, 'expert', axis=0, tiled=True)  73.8 us
    all_to_all x1, waiting for transfers between devices, dense_shards(): lax.all_to_all(hidden_grad.reshape(peer_count, token_rows, hidden_count),...  26.1 us
    all_gather x1, blocking collectives, dense_shards(): all_prob = lax.all_gather(gate_prob, 'expert', axis=0, tiled=True)  22.2 us
    all_gather x1, blocking collectives, dense_shards(): all_routes = lax.all_gather(routes, 'expert', axis=0, tiled=True)  16.4 us
    all_gather x1, waiting for transfers between devices, dense_shards(): all_hidden = lax.all_gather(hidden, 'expert', axis=0, tiled=True)  14.7 us
    dot_general x1, matrix products, expert_work(): lax.dot_general(hidden_rows, scaled_rows, dims_outer, preferred_element_t...  6.62 us
    dot_general x1, matrix products, expert_work(): lax.dot_general(scaled_rows, full_weight, dims_back, preferred_element_ty...  6.31 us
    all_to_all x1, starting transfers between devices, dense_shards(): lax.all_to_all(hidden_grad.reshape(peer_count, token_rows, hidden_count),...  5.77 us
  transfers between devices with their start and end apart: 5, of which 4 were waited for; matrix products, arithmetic and copies ran while one was open for 8% of the time, Pallas kernels for 0%

profile of v1, /device:TPU:0, one launch (start us, length us, event | category | flops | bytes accessed | tf_op | source)
XLA Modules:
  0.0 196.3 jit_solution(1898155646652865457)
XLA Ops:
  7.2 0.0 all-gather.7.cloned.1.call-start
  7.2 1.4 copy.23
  8.6 0.1 fusion.20
  8.7 0.8 fusion.14
  9.6 0.0 all-gather.7.cloned.1.call-update
  9.6 0.0 all-gather.5.cloned.1.call-start
  9.6 0.7 all-gather.5.cloned.1.call-update
  10.3 0.0 all-gather.9.cloned.1.call-start
  10.4 0.7 all-gather.9.cloned.1.call-update
  11.1 0.0 reduce-scatter.2.cloned.1.call-start
  11.1 22.2 %all_gather.16 = f32[1024,2]{0,1:T(2,128)S(1)} all-gather(f32[128,2]{0,1:T(2,128)S(1)} %copy-done.1), channel_id=1, replica_groups=mesh['groups'=2,'expert'=8,'dp'=2] {'expert'}, dimensions={0}, use_global_device_ids=true | all-gather | bytes 9216 | tf_op jit(solution)/shard_map/all_gather | solution.py:114
  33.4 16.4 %all_gather.15 = s32[1024,2]{0,1:T(2,128)S(1)} all-gather(s32[128,2]{0,1:T(2,128)S(1)} %copy-done), channel_id=1, replica_groups=mesh['groups'=2,'expert'=8,'dp'=2] {'expert'}, dimensions={0}, use_global_device_ids=true | all-gather | bytes 9216 | tf_op jit(solution)/shard_map/all_gather | solution.py:113
  49.8 14.7 %all-gather.7.cloned.1.call-done = bf16[1024,1024]{0,1:T(8,128)(2,1)} async-done(((bf16[128,1024]{0,1:T(8,128)(2,1)}), bf16[1024,1024]{0,1:T(8,128)(2,1)}) %all-gather.7.cloned.1.call-update) | async-done | bytes 2097168 | tf_op jit(solution)/shard_map/all_gather | solution.py:116
  64.5 73.8 %all-gather.5.cloned.1.call-done = bf16[1024,2048]{1,0:T(8,128)(2,1)} async-done(((bf16[128,2048]{1,0:T(8,128)(2,1)}), bf16[1024,2048]{1,0:T(8,128)(2,1)}) %all-gather.5.cloned.1.call-update) | async-done | bytes 4194320 | tf_op jit(solution)/shard_map/all_gather | solution.py:115
  138.2 6.6 %convolution_convert_fusion = bf16[512,2048]{1,0:T(8,128)(2,1)} fusion(bf16[1024,2048]{1,0:T(8,128)(2,1)} %all-gather.5.cloned.1.call-done, f32[1024]{0:T(1024)S(1)} %get-tuple-element.6, bf16[1024,1024]{0,1:T(8,128)(2,1)} %all-gather.7.cloned.1.call-done, pred[1024]{0:T(1024)(128)(4,1)S(1)} %get-tuple-element.5, pred[1024]{0:T(1024)(128)(4,1)S(1)} %get-tuple-element.4), kind=kOutput, calls=%fused_computation.1 | convolution fusion | flops 2155872256 | bytes 8394752 | tf_op jit(solution)/shard_map/dot_general | solution.py:36
  144.9 3.8 %all-gather.9.cloned.1.call-done = bf16[1,512,2048]{2,1,0:T(8,128)(2,1)} async-done(((bf16[1,256,2048]{2,1,0:T(8,128)(2,1)}), bf16[1,512,2048]{2,1,0:T(8,128)(2,1)}) %all-gather.9.cloned.1.call-update) | async-done | bytes 2097168 | tf_op jit(solution)/shard_map/all_gather | solution.py:117
  148.7 6.3 %fusion.2 = bf16[1024,512]{1,0:T(8,128)(2,1)} fusion(bf16[1,512,2048]{2,1,0:T(8,128)(2,1)} %all-gather.9.cloned.1.call-done, bf16[1024,2048]{1,0:T(8,128)(2,1)} %all-gather.5.cloned.1.call-done, f32[1024]{0:T(1024)S(1)} %get-tuple-element.6), kind=kOutput, calls=%fused_computation.4 | convolution fusion | flops 2154299392 | bytes 7344128 | tf_op jit(solution)/shard_map/dot_general | solution.py:33
  155.0 5.8 %all-to-all-start = ((bf16[8,128,512]{2,1,0:T(8,128)(2,1)}), bf16[8,128,512]{2,1,0:T(8,128)(2,1)S(1)}, u32[]{:S(2)}, u32[]{:S(2)}) async-start(bf16[8,128,512]{2,1,0:T(8,128)(2,1)} %bitcast.1), calls=%async_computation | async-start | bytes 2097152 | tf_op jit(solution)/shard_map/all_to_all | solution.py:127
  160.8 0.1 convert_element_type.34
  160.8 26.1 %all-to-all-done = bf16[8,128,512]{2,1,0:T(8,128)(2,1)S(1)} async-done(((bf16[8,128,512]{2,1,0:T(8,128)(2,1)}), bf16[8,128,512]{2,1,0:T(8,128)(2,1)S(1)}, u32[]{:S(2)}, u32[]{:S(2)}) %all-to-all-start) | async-done | bytes 1048608 | tf_op jit(solution)/shard_map/all_to_all | solution.py:127
  187.0 0.1 slice_bitcast_fusion.7
  187.1 0.1 copy.15
  187.2 0.1 copy.22
  187.3 0.1 copy.21
  187.5 0.1 copy.20
  187.6 0.1 copy.19
  187.7 0.1 copy.18
  187.9 0.1 copy.17
  188.0 0.1 copy.16
  188.1 0.5 fusion.12
  188.6 0.1 pad_maximum_fusion
  188.6 1.1 copy.24
  (9 shorter events, 0.1 us)
Async XLA Ops:
  7.2 4.0 %copy-start.1 = (f32[128,2]{0,1:T(2,128)S(1)}, f32[128,2]{0,1:T(2,128)}, u32[]{:S(2)}) copy-start(f32[128,2]{0,1:T(2,128)} %param.8) | copy-start | bytes 3076
  7.2 26.2 %copy-start = (s32[128,2]{0,1:T(2,128)S(1)}, s32[128,2]{0,1:T(2,128)}, u32[]{:S(2)}) copy-start(s32[128,2]{0,1:T(2,128)} %param.7) | copy-start | bytes 3076
  7.2 57.3 %all-gather.7.cloned.1.call-start = ((), (), s32[]{:S(2)}) async-start(), calls=%async_computation.3 | async-start | bytes 2359296 | tf_op jit(solution)/shard_map/all_gather | solution.py:116
  9.6 128.7 %all-gather.5.cloned.1.call-start = ((), (), s32[]{:S(2)}) async-start(), calls=%async_computation.2 | async-start | bytes 4718592 | tf_op jit(solution)/shard_map/all_gather | solution.py:115
  10.3 138.3 %all-gather.9.cloned.1.call-start = ((), (), s32[]{:S(2)}) async-start(), calls=%async_computation.5 | async-start | bytes 3145728 | tf_op jit(solution)/shard_map/all_gather | solution.py:117
  11.1 178.7 %reduce-scatter.2.cloned.1.call-start = ((), (), s32[]{:S(2)}) async-start(), calls=%async_computation.4 | async-start | bytes 3145728 | tf_op jit(solution)/shard_map/reduce_scatter | solution.py:134
  155.0 32.0 %all-to-all-start = ((bf16[8,128,512]{2,1,0:T(8,128)(2,1)}), bf16[8,128,512]{2,1,0:T(8,128)(2,1)S(1)}, u32[]{:S(2)}, u32[]{:S(2)}) async-start(bf16[8,128,512]{2,1,0:T(8,128)(2,1)} %bitcast.1), calls=%async_computation | async-start | bytes 2097152 | tf_op jit(solution)/shard_map/all_to_all | solution.py:127
Sparse Core Ops, SparseCore 0:
  10.6 53.8 all-gather.6
  66.6 71.5 all-gather.4
  139.8 8.8 all-gather.8
  151.3 10.7 reduce-scatter.1

commit v2 on v0

--- a/solution.py
+++ b/solution.py
@@ -1,6 +1,10 @@
+import functools
+
 import jax
 import jax.numpy as jnp
 from jax import lax
+from jax.experimental import pallas as pl
+from jax.experimental.pallas import tpu as pltpu
 from jax.sharding import PartitionSpec as P
 
 
@@ -49,7 +53,7 @@
     return (hidden_grad.reshape(peer_count, capacity, hidden_grad.shape[1]), partial_value)
 
 
-def shards(grad_out, pre_act, routes, gate_prob, down_weight):
+def packed_shards(grad_out, pre_act, routes, gate_prob, down_weight):
     peer_count = lax.axis_size("expert")
     token_rows = routes.shape[0]
     route_width = routes.shape[1]
@@ -102,6 +106,394 @@
     return (d_pre.reshape(token_rows, route_width, 2, hidden_count), summed[None])
 
 
+CHUNKS = 2
+TILE = 512
+MESH = pl.DeviceIdType.MESH
+
+
+def source_at(z, turn, planes):
+    reach = jnp.minimum(z, planes - 1 - z)
+    step = (turn + 1) // 2
+    near = jnp.where(turn % 2 == 1, z - step, z + step)
+    far = jnp.where(2 * z <= planes - 1, turn, planes - 1 - turn)
+    return jnp.where(turn <= 2 * reach, near, far)
+
+
+def dense_kernel(
+    peers,
+    grad_ref,
+    pre_ref,
+    meta_ref,
+    weight_ref,
+    d_pre_ref,
+    down_ref,
+    tokens,
+    hiddens,
+    cross_out,
+    cross_in,
+    metas,
+    columns,
+    weight,
+    chosen,
+    back_sum,
+    back_out,
+    back_in,
+    total,
+    half_out,
+    half_in,
+    zg_send,
+    zg_recv,
+    zh_send,
+    zh_recv,
+    xg_send,
+    xg_recv,
+    xh_send,
+    xh_recv,
+    back_send,
+    back_recv,
+    meta_send,
+    meta_recv,
+    dp_send,
+    dp_recv,
+):
+    planes = peers // 2
+    me = lax.axis_index("expert")
+    core = lax.axis_index("dp")
+    z, x = me // 2, me % 2
+    across = z * 2 + 1 - x
+    rows, width = grad_ref.shape
+    units = weight.shape[0]
+    half = units // 2
+    part = rows // CHUNKS
+    low = pl.multiple_of(core * half, half)
+    other = pl.multiple_of((1 - core) * half, half)
+
+    def remote(src, dst, send, recv, where):
+        return pltpu.make_async_remote_copy(
+            src_ref=src,
+            dst_ref=dst,
+            send_sem=send,
+            recv_sem=recv,
+            device_id=where,
+            device_id_type=MESH,
+        )
+
+    def z_copies(source, way, k):
+        slot = source * 2 + x
+        span = pl.ds(k * part, part)
+        to = {"expert": me + 2 if way == 0 else me - 2}
+        return (
+            remote(
+                tokens.at[slot, span], tokens.at[slot, span],
+                zg_send.at[source, way, k], zg_recv.at[source, k], to,
+            ),
+            remote(
+                hiddens.at[slot, span], hiddens.at[slot, span],
+                zh_send.at[source, way, k], zh_recv.at[source, k], to,
+            ),
+        )
+
+    def x_tokens(source, k, column):
+        slot = source * 2 + column
+        span = pl.ds(k * part, part)
+        return remote(
+            tokens.at[slot, span], tokens.at[slot, span],
+            xg_send.at[source, k], xg_recv.at[source, k], {"expert": across},
+        )
+
+    def x_hidden(source, k):
+        span = pl.ds(k * part, part)
+        return remote(
+            cross_out.at[source, span], cross_in.at[source, span],
+            xh_send.at[source, k], xh_recv.at[source, k], {"expert": across},
+        )
+
+    def back_copy(slot):
+        return remote(
+            back_out.at[slot], back_in.at[me], back_send.at[slot], back_recv.at[me], {"expert": slot}
+        )
+
+    def meta_copy(slot):
+        return remote(
+            metas.at[me], metas.at[me], meta_send.at[slot], meta_recv.at[me], {"expert": slot}
+        )
+
+    def weight_copy():
+        return remote(
+            weight_ref, weight.at[pl.ds(low, half)], dp_send.at[0], dp_recv.at[0], {"dp": 1 - core}
+        )
+
+    def half_copy():
+        return remote(half_out, half_in, dp_send.at[1], dp_recv.at[1], {"dp": 1 - core})
+
+    def moves_up(source):
+        return jnp.logical_and(source <= z, z < planes - 1)
+
+    def moves_down(source):
+        return jnp.logical_and(source >= z, z > 0)
+
+    def each_peer(body):
+        def step(slot, carry):
+            @pl.when(slot != me)
+            def _():
+                body(slot)
+
+            return carry
+
+        lax.fori_loop(0, peers, step, 0)
+
+    barrier = pltpu.get_barrier_semaphore()
+    each_peer(
+        lambda slot: pl.semaphore_signal(
+            barrier, inc=1, device_id={"expert": slot}, device_id_type=MESH
+        )
+    )
+    pl.semaphore_signal(barrier, inc=1, device_id={"dp": 1 - core}, device_id_type=MESH)
+
+    metas[me] = meta_ref[...]
+    tokens[me] = grad_ref[...]
+    for route in range(2):
+        base = route * 2 * units
+        gate = pre_ref[:, base : base + units].astype(jnp.float32)
+        up = pre_ref[:, base + units : base + 2 * units].astype(jnp.float32)
+        hiddens[me, :, route * units : (route + 1) * units] = gate_hidden(gate, up)
+
+    pl.semaphore_wait(barrier, peers)
+    each_peer(lambda slot: meta_copy(slot).start())
+
+    def pick(slot, k, expert):
+        span = pl.ds(k * part, part)
+        table = columns[slot, span]
+        wanted = expert.astype(jnp.float32)
+        first = hiddens[slot, span, :units].astype(jnp.float32)
+        second = hiddens[slot, span, units:].astype(jnp.float32)
+        rest = jnp.where(table[:, 1:2] == wanted, second, 0.0)
+        return jnp.where(table[:, 0:1] == wanted, first, rest).astype(jnp.bfloat16)
+
+    def forward_z(source, k):
+        @pl.when(moves_up(source))
+        def _():
+            for copy in z_copies(source, 0, k):
+                copy.start()
+
+        @pl.when(moves_down(source))
+        def _():
+            for copy in z_copies(source, 1, k):
+                copy.start()
+
+    for k in range(CHUNKS):
+        forward_z(z, k)
+        x_tokens(z, k, x).start()
+    weight_copy().start()
+    weight[pl.ds(low, half)] = weight_ref[...]
+    total[...] = jnp.zeros_like(total)
+    columns[me] = jnp.transpose(metas[me])
+
+    def take_meta(slot):
+        remote(
+            metas.at[slot], metas.at[slot], meta_send.at[slot], meta_recv.at[slot], {"expert": slot}
+        ).wait_recv()
+        columns[slot] = jnp.transpose(metas[slot])
+
+    each_peer(take_meta)
+    remote(
+        weight_ref, weight.at[pl.ds(other, half)], dp_send.at[0], dp_recv.at[0], {"dp": 1 - core}
+    ).wait_recv()
+
+    def work(slot):
+        table = columns[slot]
+        wanted = me.astype(jnp.float32)
+        factor = jnp.where(
+            table[:, 0:1] == wanted,
+            table[:, 2:3],
+            jnp.where(table[:, 1:2] == wanted, table[:, 3:4], 0.0),
+        )
+        back_sum[...] = jnp.zeros_like(back_sum)
+
+        def tile(j, carry):
+            span = pl.ds(pl.multiple_of(j * TILE, TILE), TILE)
+            scaled = (factor * tokens[slot, :, span].astype(jnp.float32)).astype(jnp.bfloat16)
+            total[:, span] += lax.dot_general(
+                chosen[...], scaled, (((0,), (0,)), ((), ())), preferred_element_type=jnp.float32
+            )
+            back_sum[...] += lax.dot_general(
+                scaled, weight[:, span], (((1,), (1,)), ((), ())), preferred_element_type=jnp.float32
+            )
+            return carry
+
+        lax.fori_loop(0, width // TILE, tile, 0)
+
+        @pl.when(slot == me)
+        def _():
+            back_in[me] = back_sum[...].astype(jnp.bfloat16)
+
+        @pl.when(slot != me)
+        def _():
+            back_out[slot] = back_sum[...].astype(jnp.bfloat16)
+            back_copy(slot).start()
+
+    def turn_step(turn, carry):
+        @pl.when(turn < planes)
+        def _():
+            source = source_at(z, turn, planes)
+            slot = source * 2 + x
+            for k in range(CHUNKS):
+                @pl.when(turn > 0)
+                def _():
+                    for copy in z_copies(source, 0, k):
+                        copy.wait_recv()
+                    forward_z(source, k)
+                    x_tokens(source, k, x).start()
+
+                span = pl.ds(k * part, part)
+                cross_out[source, span] = pick(slot, k, across)
+                x_hidden(source, k).start()
+
+        def side(column, inner):
+            @pl.when(jnp.logical_and(column == 0, turn < planes))
+            def _():
+                slot = source_at(z, turn, planes) * 2 + x
+                for k in range(CHUNKS):
+                    chosen[pl.ds(k * part, part)] = pick(slot, k, me)
+
+            @pl.when(jnp.logical_and(column == 1, turn > 0))
+            def _():
+                source = source_at(z, turn - 1, planes)
+                for k in range(CHUNKS):
+                    x_tokens(source, k, 1 - x).wait_recv()
+                    x_hidden(source, k).wait_recv()
+                chosen[...] = cross_in[source]
+
+            @pl.when(jnp.where(column == 0, turn < planes, turn > 0))
+            def _():
+                source = source_at(z, turn - column, planes)
+                work(source * 2 + (x + column) % 2)
+
+            return inner
+
+        return lax.fori_loop(0, 2, side, carry)
+
+    lax.fori_loop(0, planes + 1, turn_step, 0)
+
+    half_out[...] = total[pl.ds(other, half)].astype(jnp.bfloat16)
+    half_copy().start()
+
+    each_peer(
+        lambda slot: remote(
+            back_out.at[slot], back_in.at[slot], back_send.at[slot], back_recv.at[slot],
+            {"expert": slot},
+        ).wait_recv()
+    )
+    mine = columns[me]
+    for route in range(2):
+        def gather(slot, carry):
+            hit = mine[:, route : route + 1] == slot.astype(jnp.float32)
+            back_sum[...] = jnp.where(hit, back_in[slot].astype(jnp.float32), back_sum[...])
+            return carry
+
+        lax.fori_loop(0, peers, gather, 0)
+        base = route * 2 * units
+        gate = pre_ref[:, base : base + units].astype(jnp.float32)
+        up = pre_ref[:, base + units : base + 2 * units].astype(jnp.float32)
+        d_pre_ref[:, base : base + 2 * units] = activation_grads(back_sum[...], gate, up)
+
+    half_copy().wait_recv()
+    kept = total[pl.ds(low, half)].astype(jnp.bfloat16).astype(jnp.float32)
+    down_ref[...] = (kept + half_in[...].astype(jnp.float32)).astype(jnp.bfloat16)
+
+    weight_copy().wait_send()
+    half_copy().wait_send()
+
+    def drain(slot):
+        back_copy(slot).wait_send()
+        meta_copy(slot).wait_send()
+
+    each_peer(drain)
+
+    def drain_plane(source, carry):
+        for k in range(CHUNKS):
+            x_tokens(source, k, x).wait_send()
+            x_hidden(source, k).wait_send()
+
+            @pl.when(moves_up(source))
+            def _():
+                for copy in z_copies(source, 0, k):
+                    copy.wait_send()
+
+            @pl.when(moves_down(source))
+            def _():
+                for copy in z_copies(source, 1, k):
+                    copy.wait_send()
+
+        return carry
+
+    lax.fori_loop(0, planes, drain_plane, 0)
+
+
+def dense_shards(grad_out, pre_act, routes, gate_prob, down_weight):
+    peers = lax.axis_size("expert")
+    planes = peers // 2
+    rows, width = grad_out.shape
+    units = pre_act.shape[3]
+    half = down_weight.shape[1]
+    meta = jnp.concatenate([routes.astype(jnp.float32), gate_prob], axis=1).T
+    meta = jnp.concatenate([meta, jnp.zeros_like(meta)], axis=0)
+    whole = pl.BlockSpec(memory_space=pltpu.VMEM)
+    dma = pltpu.SemaphoreType.DMA
+    bf16, f32 = jnp.bfloat16, jnp.float32
+    d_pre, grad_down = pl.pallas_call(
+        functools.partial(dense_kernel, peers),
+        out_shape=(
+            jax.ShapeDtypeStruct((rows, 4 * units), bf16),
+            jax.ShapeDtypeStruct((half, width), bf16),
+        ),
+        in_specs=[whole] * 4,
+        out_specs=(whole, whole),
+        scratch_shapes=[
+            pltpu.VMEM((peers, rows, width), bf16),
+            pltpu.VMEM((peers, rows, 2 * units), bf16),
+            pltpu.VMEM((planes, rows, units), bf16),
+            pltpu.VMEM((planes, rows, units), bf16),
+            pltpu.VMEM((peers, 8, rows), f32),
+            pltpu.VMEM((peers, rows, 8), f32),
+            pltpu.VMEM((units, width), bf16),
+            pltpu.VMEM((rows, units), bf16),
+            pltpu.VMEM((rows, units), f32),
+            pltpu.VMEM((peers, rows, units), bf16),
+            pltpu.VMEM((peers, rows, units), bf16),
+            pltpu.VMEM((units, width), f32),
+            pltpu.VMEM((half, width), bf16),
+            pltpu.VMEM((half, width), bf16),
+            dma((planes, 2, CHUNKS)),
+            dma((planes, CHUNKS)),
+            dma((planes, 2, CHUNKS)),
+            dma((planes, CHUNKS)),
+            dma((planes, CHUNKS)),
+            dma((planes, CHUNKS)),
+            dma((planes, CHUNKS)),
+            dma((planes, CHUNKS)),
+            dma((peers,)),
+            dma((peers,)),
+            dma((peers,)),
+            dma((peers,)),
+            dma((2,)),
+            dma((2,)),
+        ],
+        compiler_params=pltpu.CompilerParams(
+            collective_id=0, has_side_effects=True, vmem_limit_bytes=48 * 1024 * 1024
+        ),
+    )(grad_out, pre_act.reshape(rows, 4 * units), meta, down_weight[0])
+    return (d_pre.reshape(rows, 2, 2, units), grad_down[None])
+
+
+def shards(grad_out, pre_act, routes, gate_prob, down_weight):
+    peers, cores = lax.axis_size("expert"), lax.axis_size("dp")
+    capacity = 4 * routes.shape[0] * routes.shape[1] // peers
+    dense = capacity >= routes.shape[0] and peers % 2 == 0 and cores == 2
+    plan = dense_shards if dense else packed_shards
+    return plan(grad_out, pre_act, routes, gate_prob, down_weight)
+
+
 def solution(mesh):
     placed = (
         P(("groups", "expert", "dp"), None),

time: 245 us -> 100 us (0.41)
  the two profiles are of different devices: /device:TPU:0 before, /device:TPU:28 now
where the time goes in v2:
time: 100 us
  Pallas kernels  93.4 us (93%)
  local copies, waits for them, and re-layouts  4.61 us (5%)
  other arithmetic  1.46 us (1%)
    pallas_call x1, Pallas kernels, dense_shards(): pl.pallas_call(functools.partial(dense_kernel, peers), out_shape=(jax.Sha...  93.4 us
    unnamed x5, local copies, waits for them, and re-layouts  2.01 us

profile of v2, /device:TPU:28, one launch (start us, length us, event | category | flops | bytes accessed | tf_op | source)
XLA Modules:
  0.0 100.1 jit_solution(4852235050207174958)
XLA Ops:
  0.6 0.0 copy-start
  0.6 0.8 convert_element_type.3
  1.4 0.7 maximum_bitcast_fusion
  2.1 1.4 %reshape.10.pre_ref = bf16[128,2048]{1,0:T(8,128)(2,1)S(1)} reshape(bf16[128,2,2,512]{3,2,1,0:T(2,128)(2,1)} %param.6) | data formatting | bytes 1048576 | tf_op jit(solution)/shard_map/reshape | solution.py:485
  3.5 0.0 copy-done
  3.5 0.0 copy-start.1
  3.6 1.0 %copy-done.1 = bf16[128,2048]{1,0:T(8,128)(2,1)S(1)} copy-done((bf16[128,2048]{1,0:T(8,128)(2,1)S(1)}, bf16[128,2048]{1,0:T(8,128)(2,1)}, u32[]{:S(2)}) %copy-start.1) | copy-done | bytes 524312
  4.6 93.4 %shard_map.68 = (bf16[128,2048]{1,0:T(8,128)(2,1)S(1)}, bf16[256,2048]{1,0:T(8,128)(2,1)S(1)}) custom-call(bf16[128,2048]{1,0:T(8,128)(2,1)S(1)} %copy-done.1, bf16[128,2048]{1,0:T(8,128)(2,1)S(1)} %reshape.10.pre_ref, f32[8,128]{1,0:T(8,128)S(1)} %concatenate.7.meta_ref, bf16[256,2048]{1,0:T(8,128)(2,1)S(1)} %bitcast.4), custom_call_target="tpu_custom_call" | custom-call | tf_op jit(solution)/shard_map/pallas_call | solution.py:444
  98.0 1.2 %reshape.11 = bf16[128,2,2,512]{3,2,1,0:T(2,128)(2,1)} reshape(bf16[128,2048]{1,0:T(8,128)(2,1)S(1)} %get-tuple-element.4) | data formatting | bytes 1048576 | tf_op jit(solution)/shard_map/reshape | solution.py:486
  99.2 1.0 copy.8
  (1 shorter events, 0.0 us)
Async XLA Ops:
  0.6 2.9 %copy-start = (bf16[1,256,2048]{2,1,0:T(8,128)(2,1)S(1)}, bf16[1,256,2048]{2,1,0:T(8,128)(2,1)}, u32[]{:S(2)}) copy-start(bf16[1,256,2048]{2,1,0:T(8,128)(2,1)} %param.9) | copy-start | bytes 3145732
  3.5 1.0 %copy-start.1 = (bf16[128,2048]{1,0:T(8,128)(2,1)S(1)}, bf16[128,2048]{1,0:T(8,128)(2,1)}, u32[]{:S(2)}) copy-start(bf16[128,2048]{1,0:T(8,128)(2,1)} %grad_ref.1) | copy-start | bytes 1572868

commit v3 on v2

--- a/solution.py
+++ b/solution.py
@@ -106,7 +106,7 @@
     return (d_pre.reshape(token_rows, route_width, 2, hidden_count), summed[None])
 
 
-CHUNKS = 2
+CHUNKS = 4
 TILE = 512
 MESH = pl.DeviceIdType.MESH
 
@@ -123,7 +123,8 @@
     peers,
     grad_ref,
     pre_ref,
-    meta_ref,
+    routes_ref,
+    prob_ref,
     weight_ref,
     d_pre_ref,
     down_ref,
@@ -155,6 +156,7 @@
     meta_recv,
     dp_send,
     dp_recv,
+    load_sem,
 ):
     planes = peers // 2
     me = lax.axis_index("expert")
@@ -220,7 +222,7 @@
 
     def weight_copy():
         return remote(
-            weight_ref, weight.at[pl.ds(low, half)], dp_send.at[0], dp_recv.at[0], {"dp": 1 - core}
+            weight.at[pl.ds(low, half)], weight.at[pl.ds(low, half)], dp_send.at[0], dp_recv.at[0], {"dp": 1 - core}
         )
 
     def half_copy():
@@ -250,8 +252,15 @@
     )
     pl.semaphore_signal(barrier, inc=1, device_id={"dp": 1 - core}, device_id_type=MESH)
 
-    metas[me] = meta_ref[...]
-    tokens[me] = grad_ref[...]
+    metas[me] = jnp.zeros((8, rows), jnp.float32)
+    metas[me, 0:2] = routes_ref[...].astype(jnp.float32)
+    metas[me, 2:4] = prob_ref[...]
+    load_tokens = pltpu.make_async_copy(grad_ref, tokens.at[me], load_sem.at[0])
+    load_tokens.start()
+    load_weight = pltpu.make_async_copy(
+        weight_ref, weight.at[pl.ds(low, half)], load_sem.at[1]
+    )
+    load_weight.start()
     for route in range(2):
         base = route * 2 * units
         gate = pre_ref[:, base : base + units].astype(jnp.float32)
@@ -259,6 +268,7 @@
         hiddens[me, :, route * units : (route + 1) * units] = gate_hidden(gate, up)
 
     pl.semaphore_wait(barrier, peers)
+    load_tokens.wait()
     each_peer(lambda slot: meta_copy(slot).start())
 
     def pick(slot, k, expert):
@@ -284,8 +294,8 @@
     for k in range(CHUNKS):
         forward_z(z, k)
         x_tokens(z, k, x).start()
+    load_weight.wait()
     weight_copy().start()
-    weight[pl.ds(low, half)] = weight_ref[...]
     total[...] = jnp.zeros_like(total)
     columns[me] = jnp.transpose(metas[me])
 
@@ -297,10 +307,10 @@
 
     each_peer(take_meta)
     remote(
-        weight_ref, weight.at[pl.ds(other, half)], dp_send.at[0], dp_recv.at[0], {"dp": 1 - core}
+        weight.at[pl.ds(other, half)], weight.at[pl.ds(other, half)], dp_send.at[0], dp_recv.at[0], {"dp": 1 - core}
     ).wait_recv()
 
-    def work(slot):
+    def work(slot, now):
         table = columns[slot]
         wanted = me.astype(jnp.float32)
         factor = jnp.where(
@@ -330,7 +340,10 @@
         @pl.when(slot != me)
         def _():
             back_out[slot] = back_sum[...].astype(jnp.bfloat16)
-            back_copy(slot).start()
+
+            @pl.when(now)
+            def _():
+                back_copy(slot).start()
 
     def turn_step(turn, carry):
         @pl.when(turn < planes)
@@ -349,6 +362,19 @@
                 cross_out[source, span] = pick(slot, k, across)
                 x_hidden(source, k).start()
 
+        @pl.when(turn == planes - 1)
+        def _():
+            def release(index, carry):
+                slot = source_at(z, index // 2, planes) * 2 + (x + index % 2) % 2
+
+                @pl.when(slot != me)
+                def _():
+                    back_copy(slot).start()
+
+                return carry
+
+            lax.fori_loop(0, 2 * planes - 3, release, 0)
+
         def side(column, inner):
             @pl.when(jnp.logical_and(column == 0, turn < planes))
             def _():
@@ -367,7 +393,7 @@
             @pl.when(jnp.where(column == 0, turn < planes, turn > 0))
             def _():
                 source = source_at(z, turn - column, planes)
-                work(source * 2 + (x + column) % 2)
+                work(source * 2 + (x + column) % 2, turn >= planes - 1)
 
             return inner
 
@@ -436,9 +462,8 @@
     rows, width = grad_out.shape
     units = pre_act.shape[3]
     half = down_weight.shape[1]
-    meta = jnp.concatenate([routes.astype(jnp.float32), gate_prob], axis=1).T
-    meta = jnp.concatenate([meta, jnp.zeros_like(meta)], axis=0)
     whole = pl.BlockSpec(memory_space=pltpu.VMEM)
+    away = pl.BlockSpec(memory_space=pl.ANY)
     dma = pltpu.SemaphoreType.DMA
     bf16, f32 = jnp.bfloat16, jnp.float32
     d_pre, grad_down = pl.pallas_call(
@@ -447,7 +472,7 @@
             jax.ShapeDtypeStruct((rows, 4 * units), bf16),
             jax.ShapeDtypeStruct((half, width), bf16),
         ),
-        in_specs=[whole] * 4,
+        in_specs=[away, whole, whole, whole, away],
         out_specs=(whole, whole),
         scratch_shapes=[
             pltpu.VMEM((peers, rows, width), bf16),
@@ -478,11 +503,12 @@
             dma((peers,)),
             dma((2,)),
             dma((2,)),
+            dma((2,)),
         ],
         compiler_params=pltpu.CompilerParams(
             collective_id=0, has_side_effects=True, vmem_limit_bytes=48 * 1024 * 1024
         ),
-    )(grad_out, pre_act.reshape(rows, 4 * units), meta, down_weight[0])
+    )(grad_out, pre_act.reshape(rows, 4 * units), routes.T, gate_prob.T, down_weight[0])
     return (d_pre.reshape(rows, 2, 2, units), grad_down[None])
 
 

time: 100 us -> 92.3 us (0.923)
  the two profiles are of different devices: /device:TPU:28 before, /device:TPU:0 now
where the time goes in v3:
time: 92.3 us; the launch traced here: 92.1 us
  Pallas kernels  86.7 us (94%)
  local copies, waits for them, and re-layouts  4.69 us (5%)
    pallas_call x1, Pallas kernels, dense_shards(): pl.pallas_call(functools.partial(dense_kernel, peers), out_shape=(jax.Sha...  86.7 us
    unnamed x9, local copies, waits for them, and re-layouts  2.02 us

profile of v3, /device:TPU:0, one launch (start us, length us, event | category | flops | bytes accessed | tf_op | source)
XLA Modules:
  0.0 92.1 jit_solution(14576427764529386218)
XLA Ops:
  0.6 0.0 copy-start
  0.6 0.0 copy-start.2
  0.7 0.0 copy-start.3
  0.7 1.5 %reshape.10.pre_ref = bf16[128,2048]{1,0:T(8,128)(2,1)S(1)} reshape(bf16[128,2,2,512]{3,2,1,0:T(2,128)(2,1)} %param.6) | data formatting | bytes 1048576 | tf_op jit(solution)/shard_map/reshape | solution.py:511
  2.2 0.0 copy-done
  2.2 0.0 copy-done.2
  2.2 0.0 copy-done.3
  2.2 0.0 copy-start.1
  2.2 1.0 %copy-done.1 = bf16[128,2048]{1,0:T(8,128)(2,1)S(1)} copy-done((bf16[128,2048]{1,0:T(8,128)(2,1)S(1)}, bf16[128,2048]{1,0:T(8,128)(2,1)}, u32[]{:S(2)}) %copy-start.1) | copy-done | bytes 524312
  3.2 86.7 %shard_map.68 = (bf16[128,2048]{1,0:T(8,128)(2,1)S(1)}, bf16[256,2048]{1,0:T(8,128)(2,1)S(1)}) custom-call(bf16[128,2048]{1,0:T(8,128)(2,1)S(1)} %copy-done.1, bf16[128,2048]{1,0:T(8,128)(2,1)S(1)} %reshape.10.pre_ref, s32[2,128]{1,0:T(2,128)S(1)} %bitcast.6, f32[2,128]{1,0:T(2,128)S(1)} %bitcast.7, bf16[256,2048]{1,0:T(8,128)(2,1)S(1)} %bitcast.4), custom_call_target="tpu_custom_call" | custom-call | tf_op jit(solution)/shard_map/pallas_call | solution.py:469
  90.0 1.2 %reshape.11 = bf16[128,2,2,512]{3,2,1,0:T(2,128)(2,1)} reshape(bf16[128,2048]{1,0:T(8,128)(2,1)S(1)} %get-tuple-element.4) | data formatting | bytes 1048576 | tf_op jit(solution)/shard_map/reshape | solution.py:512
  91.1 1.0 %copy.8 = bf16[1,256,2048]{2,1,0:T(8,128)(2,1)} copy(bf16[1,256,2048]{2,1,0:T(8,128)(2,1)S(1)} %bitcast.5) | data formatting | bytes 2097152
Async XLA Ops:
  0.6 1.5 %copy-start = (bf16[1,256,2048]{2,1,0:T(8,128)(2,1)S(1)}, bf16[1,256,2048]{2,1,0:T(8,128)(2,1)}, u32[]{:S(2)}) copy-start(bf16[1,256,2048]{2,1,0:T(8,128)(2,1)} %param.9) | copy-start | bytes 3145732
  0.6 1.5 %copy-start.2 = (s32[128,2]{0,1:T(2,128)S(1)}, s32[128,2]{0,1:T(2,128)}, u32[]{:S(2)}) copy-start(s32[128,2]{0,1:T(2,128)} %param.7) | copy-start | bytes 3076
  0.7 1.5 %copy-start.3 = (f32[128,2]{0,1:T(2,128)S(1)}, f32[128,2]{0,1:T(2,128)}, u32[]{:S(2)}) copy-start(f32[128,2]{0,1:T(2,128)} %param.8) | copy-start | bytes 3076
  2.2 1.0 %copy-start.1 = (bf16[128,2048]{1,0:T(8,128)(2,1)S(1)}, bf16[128,2048]{1,0:T(8,128)(2,1)}, u32[]{:S(2)}) copy-start(bf16[128,2048]{1,0:T(8,128)(2,1)} %grad_ref.1) | copy-start | bytes 1572868

commit v4 on v3

--- a/solution.py
+++ b/solution.py
@@ -114,8 +114,10 @@
 def source_at(z, turn, planes):
     reach = jnp.minimum(z, planes - 1 - z)
     step = (turn + 1) // 2
-    near = jnp.where(turn % 2 == 1, z - step, z + step)
-    far = jnp.where(2 * z <= planes - 1, turn, planes - 1 - turn)
+    lower = 2 * z <= planes - 1
+    odd = jnp.where(turn % 2 == 1, 1, -1)
+    near = jnp.where(lower, z + odd * step, z - odd * step)
+    far = jnp.where(lower, turn, planes - 1 - turn)
     return jnp.where(turn <= 2 * reach, near, far)
 
 
@@ -345,6 +347,11 @@
             def _():
                 back_copy(slot).start()
 
+    edge = jnp.logical_or(z == 0, z == planes - 1)
+
+    def now_at(turn):
+        return jnp.logical_or(edge, turn >= planes - 1)
+
     def turn_step(turn, carry):
         @pl.when(turn < planes)
         def _():
@@ -362,7 +369,7 @@
                 cross_out[source, span] = pick(slot, k, across)
                 x_hidden(source, k).start()
 
-        @pl.when(turn == planes - 1)
+        @pl.when(jnp.logical_and(turn == planes - 1, jnp.logical_not(edge)))
         def _():
             def release(index, carry):
                 slot = source_at(z, index // 2, planes) * 2 + (x + index % 2) % 2
@@ -393,7 +400,7 @@
             @pl.when(jnp.where(column == 0, turn < planes, turn > 0))
             def _():
                 source = source_at(z, turn - column, planes)
-                work(source * 2 + (x + column) % 2, turn >= planes - 1)
+                work(source * 2 + (x + column) % 2, now_at(turn))
 
             return inner
 

time: 92.3 us -> 88.9 us (0.963)
  Pallas kernels: 86.7 us -> 83.4 us
    pallas_call x1, Pallas kernels: 86.7 us -> 83.4 us  [dense_shards(): pl.pallas_call(functools.partial(dense_kernel, peers), out_shape=(jax.Sha...]
where the time goes in v4:
time: 88.9 us; the launch traced here: 88.8 us
  Pallas kernels  83.4 us (94%)
  local copies, waits for them, and re-layouts  4.69 us (5%)
    pallas_call x1, Pallas kernels, dense_shards(): pl.pallas_call(functools.partial(dense_kernel, peers), out_shape=(jax.Sha...  83.4 us
    unnamed x9, local copies, waits for them, and re-layouts  2.02 us

profile of v4, /device:TPU:0, one launch (start us, length us, event | category | flops | bytes accessed | tf_op | source)
XLA Modules:
  0.0 88.8 jit_solution(11073186806900544347)
XLA Ops:
  0.6 0.0 copy-start
  0.6 0.0 copy-start.2
  0.7 0.0 copy-start.3
  0.7 1.5 %reshape.10.pre_ref = bf16[128,2048]{1,0:T(8,128)(2,1)S(1)} reshape(bf16[128,2,2,512]{3,2,1,0:T(2,128)(2,1)} %param.6) | data formatting | bytes 1048576 | tf_op jit(solution)/shard_map/reshape | solution.py:518
  2.2 0.0 copy-done
  2.2 0.0 copy-done.2
  2.2 0.0 copy-done.3
  2.2 0.0 copy-start.1
  2.2 1.0 %copy-done.1 = bf16[128,2048]{1,0:T(8,128)(2,1)S(1)} copy-done((bf16[128,2048]{1,0:T(8,128)(2,1)S(1)}, bf16[128,2048]{1,0:T(8,128)(2,1)}, u32[]{:S(2)}) %copy-start.1) | copy-done | bytes 524312
  3.2 83.4 %shard_map.68 = (bf16[128,2048]{1,0:T(8,128)(2,1)S(1)}, bf16[256,2048]{1,0:T(8,128)(2,1)S(1)}) custom-call(bf16[128,2048]{1,0:T(8,128)(2,1)S(1)} %copy-done.1, bf16[128,2048]{1,0:T(8,128)(2,1)S(1)} %reshape.10.pre_ref, s32[2,128]{1,0:T(2,128)S(1)} %bitcast.6, f32[2,128]{1,0:T(2,128)S(1)} %bitcast.7, bf16[256,2048]{1,0:T(8,128)(2,1)S(1)} %bitcast.4), custom_call_target="tpu_custom_call" | custom-call | tf_op jit(solution)/shard_map/pallas_call | solution.py:476
  86.6 1.2 %reshape.11 = bf16[128,2,2,512]{3,2,1,0:T(2,128)(2,1)} reshape(bf16[128,2048]{1,0:T(8,128)(2,1)S(1)} %get-tuple-element.4) | data formatting | bytes 1048576 | tf_op jit(solution)/shard_map/reshape | solution.py:519
  87.8 1.0 %copy.8 = bf16[1,256,2048]{2,1,0:T(8,128)(2,1)} copy(bf16[1,256,2048]{2,1,0:T(8,128)(2,1)S(1)} %bitcast.5) | data formatting | bytes 2097152
Async XLA Ops:
  0.6 1.5 %copy-start = (bf16[1,256,2048]{2,1,0:T(8,128)(2,1)S(1)}, bf16[1,256,2048]{2,1,0:T(8,128)(2,1)}, u32[]{:S(2)}) copy-start(bf16[1,256,2048]{2,1,0:T(8,128)(2,1)} %param.9) | copy-start | bytes 3145732
  0.6 1.5 %copy-start.2 = (s32[128,2]{0,1:T(2,128)S(1)}, s32[128,2]{0,1:T(2,128)}, u32[]{:S(2)}) copy-start(s32[128,2]{0,1:T(2,128)} %param.7) | copy-start | bytes 3076
  0.7 1.5 %copy-start.3 = (f32[128,2]{0,1:T(2,128)S(1)}, f32[128,2]{0,1:T(2,128)}, u32[]{:S(2)}) copy-start(f32[128,2]{0,1:T(2,128)} %param.8) | copy-start | bytes 3076
  2.2 1.0 %copy-start.1 = (bf16[128,2048]{1,0:T(8,128)(2,1)S(1)}, bf16[128,2048]{1,0:T(8,128)(2,1)}, u32[]{:S(2)}) copy-start(bf16[128,2048]{1,0:T(8,128)(2,1)} %grad_ref.1) | copy-start | bytes 1572868

commit v5 on v4

--- a/solution.py
+++ b/solution.py
@@ -107,7 +107,7 @@
 
 
 CHUNKS = 4
-TILE = 512
+TILE = 1024
 MESH = pl.DeviceIdType.MESH
 
 

time: 88.9 us -> 88.6 us (level)
  no operation moved by 1% of the time
where the time goes in v5:
time: 88.6 us; the launch traced here: 88.4 us
  Pallas kernels  83 us (94%)
  local copies, waits for them, and re-layouts  4.69 us (5%)
    pallas_call x1, Pallas kernels, dense_shards(): pl.pallas_call(functools.partial(dense_kernel, peers), out_shape=(jax.Sha...  83 us
    unnamed x9, local copies, waits for them, and re-layouts  2.02 us

profile of v5, /device:TPU:0, one launch (start us, length us, event | category | flops | bytes accessed | tf_op | source)
XLA Modules:
  0.0 88.4 jit_solution(17346253608738426091)
XLA Ops:
  0.6 0.0 copy-start
  0.6 0.0 copy-start.2
  0.7 0.0 copy-start.3
  0.7 1.5 %reshape.10.pre_ref = bf16[128,2048]{1,0:T(8,128)(2,1)S(1)} reshape(bf16[128,2,2,512]{3,2,1,0:T(2,128)(2,1)} %param.6) | data formatting | bytes 1048576 | tf_op jit(solution)/shard_map/reshape | solution.py:518
  2.2 0.0 copy-done
  2.2 0.0 copy-done.2
  2.2 0.0 copy-done.3
  2.2 0.0 copy-start.1
  2.2 1.0 %copy-done.1 = bf16[128,2048]{1,0:T(8,128)(2,1)S(1)} copy-done((bf16[128,2048]{1,0:T(8,128)(2,1)S(1)}, bf16[128,2048]{1,0:T(8,128)(2,1)}, u32[]{:S(2)}) %copy-start.1) | copy-done | bytes 524312
  3.2 83.0 %shard_map.68 = (bf16[128,2048]{1,0:T(8,128)(2,1)S(1)}, bf16[256,2048]{1,0:T(8,128)(2,1)S(1)}) custom-call(bf16[128,2048]{1,0:T(8,128)(2,1)S(1)} %copy-done.1, bf16[128,2048]{1,0:T(8,128)(2,1)S(1)} %reshape.10.pre_ref, s32[2,128]{1,0:T(2,128)S(1)} %bitcast.6, f32[2,128]{1,0:T(2,128)S(1)} %bitcast.7, bf16[256,2048]{1,0:T(8,128)(2,1)S(1)} %bitcast.4), custom_call_target="tpu_custom_call" | custom-call | tf_op jit(solution)/shard_map/pallas_call | solution.py:476
  86.3 1.2 %reshape.11 = bf16[128,2,2,512]{3,2,1,0:T(2,128)(2,1)} reshape(bf16[128,2048]{1,0:T(8,128)(2,1)S(1)} %get-tuple-element.4) | data formatting | bytes 1048576 | tf_op jit(solution)/shard_map/reshape | solution.py:519
  87.5 1.0 %copy.8 = bf16[1,256,2048]{2,1,0:T(8,128)(2,1)} copy(bf16[1,256,2048]{2,1,0:T(8,128)(2,1)S(1)} %bitcast.5) | data formatting | bytes 2097152
Async XLA Ops:
  0.6 1.5 %copy-start = (bf16[1,256,2048]{2,1,0:T(8,128)(2,1)S(1)}, bf16[1,256,2048]{2,1,0:T(8,128)(2,1)}, u32[]{:S(2)}) copy-start(bf16[1,256,2048]{2,1,0:T(8,128)(2,1)} %param.9) | copy-start | bytes 3145732
  0.6 1.5 %copy-start.2 = (s32[128,2]{0,1:T(2,128)S(1)}, s32[128,2]{0,1:T(2,128)}, u32[]{:S(2)}) copy-start(s32[128,2]{0,1:T(2,128)} %param.7) | copy-start | bytes 3076
  0.7 1.5 %copy-start.3 = (f32[128,2]{0,1:T(2,128)S(1)}, f32[128,2]{0,1:T(2,128)}, u32[]{:S(2)}) copy-start(f32[128,2]{0,1:T(2,128)} %param.8) | copy-start | bytes 3076
  2.2 1.0 %copy-start.1 = (bf16[128,2048]{1,0:T(8,128)(2,1)S(1)}, bf16[128,2048]{1,0:T(8,128)(2,1)}, u32[]{:S(2)}) copy-start(bf16[128,2048]{1,0:T(8,128)(2,1)} %grad_ref.1) | copy-start | bytes 1572868
